TPU v7x, 32 devices: a whole 2x2x4 slice. The times are simulated.
32 devices in a mesh: gx: 8 (over y, x, core), gy: 4 (over z).
Axes of the slice: x: 2, y: 2, z: 4, core: 2. Of those that a mesh axis runs over, the one named last changes fastest.
Arguments:
- checkpoint: float32 [19, 64, 256, 128], P(None, 'gx', 'gy'), may hold values from 0 to 1, as said below
- fluid: int32 [64, 256, 128], P('gx', 'gy'), may hold values 0 or 1
- adjoint_in: float32 [19, 64, 256, 128], P(None, 'gx', 'gy'), may hold values from -6 to 6
Outputs:
- state: float32 [19, 64, 256, 128], P(None, 'gx', 'gy')
- adjoint: float32 [19, 64, 256, 128], P(None, 'gx', 'gy')
Inputs may be any that keep to these rules, and one draw needn't show every extreme that they name: `checkpoint`: positive populations near equilibrium. 1 marks a fluid cell, 0 a solid one.
All inputs are finite; a program needn't handle non-finite values. No bound on the sum of `fluid` on one device may be relied on, other than what follows from the above.
Results may differ from a plain program's by a relative error of at most 0.0003.
Values sent between devices are 32-bit elements; how exact they have to be, the bound alone decides.
A program may use at most 128 MiB of HBM per device.

v0:
```python
import jax
import jax.numpy as jnp
from jax import lax
from jax.experimental import pallas as pl
from jax.experimental.pallas import tpu as pltpu
from jax.sharding import PartitionSpec as P

VELOCITY = [
    (0, 0, 0),
    (1, 0, 0),
    (-1, 0, 0),
    (0, 1, 0),
    (0, -1, 0),
    (0, 0, 1),
    (0, 0, -1),
    (1, 1, 0),
    (-1, -1, 0),
    (1, -1, 0),
    (-1, 1, 0),
    (1, 0, 1),
    (-1, 0, -1),
    (1, 0, -1),
    (-1, 0, 1),
    (0, 1, 1),
    (0, -1, -1),
    (0, 1, -1),
    (0, -1, 1),
]
OPPOSITE = [0, 2, 1, 4, 3, 6, 5, 8, 7, 10, 9, 12, 11, 14, 13, 16, 15, 18, 17]
ORDER = [0, 1, 7, 9, 11, 13, 2, 8, 10, 12, 14, 3, 4, 5, 6, 15, 16, 17, 18]
SLOT = [ORDER.index(q) for q in range(19)]
UP = [3, 7, 10, 15, 17]
DOWN = [4, 8, 9, 16, 18]
CORNER = [7, 8, 9, 10]
PAD = 8
T = 8
MIB = 1 << 20


def shifted(ref, q, x, y, speed):
    row = PAD + T * y - speed[1]
    tile = ref[SLOT[q], x + 1 - speed[0], row : row + T, :]
    if speed[2]:
        tile = pltpu.roll(tile, speed[2] % tile.shape[1], 1)
    return tile


def own(ref, q, x, y):
    return ref[SLOT[q], x + 1, PAD + T * y : PAD + T * y + T, :]


def stream(ref, bits, x, y):
    result = [own(ref, 0, x, y)]
    for q in range(1, 19):
        is_open = (bits & (1 << q)) != 0
        result.append(
            jnp.where(is_open, shifted(ref, q, x, y, VELOCITY[q]), own(ref, OPPOSITE[q], x, y))
        )
    return result


def moments(v):
    s = {q: v[q] + v[q + 1] for q in range(1, 19, 2)}
    d = {q: v[q] - v[q + 1] for q in range(1, 19, 2)}
    rho = v[0] + ((s[1] + s[3]) + (s[5] + s[7])) + ((s[9] + s[11]) + (s[13] + (s[15] + s[17])))
    mx = d[1] + (d[7] + d[9]) + (d[11] + d[13])
    my = d[3] + (d[7] - d[9]) + (d[15] + d[17])
    mz = d[5] + (d[11] - d[13]) + (d[15] - d[17])
    return rho, mx, my, mz


def collide(v):
    rho, mx, my, mz = moments(v)
    inverse = 3.0 / rho
    ux, uy, uz = mx * inverse, my * inverse, mz * inverse
    base = 1.0 - (ux * ux + uy * uy + uz * uz) * (1.0 / 6.0)
    along = {
        1: ux,
        3: uy,
        5: uz,
        7: ux + uy,
        9: ux - uy,
        11: ux + uz,
        13: ux - uz,
        15: uy + uz,
        17: uy - uz,
    }
    axis, diagonal = rho * (1.6 / 18.0), rho * (1.6 / 36.0)
    result = [rho * (1.6 / 3.0) * base - 0.6 * v[0]]
    for q in range(1, 19, 2):
        a = along[q]
        even = base + 0.5 * (a * a)
        factor = axis if q < 7 else diagonal
        result.append(factor * (even + a) - 0.6 * v[q])
        result.append(factor * (even - a) - 0.6 * v[q + 1])
    return result


def pull_back(v, b):
    rho, mx, my, mz = moments(v)
    inverse = 1.0 / rho
    ux, uy, uz = mx * inverse, my * inverse, mz * inverse
    s = {q: b[q] + b[q + 1] for q in range(1, 19, 2)}
    d = {q: b[q] - b[q + 1] for q in range(1, 19, 2)}
    for q in (1, 3, 5):
        s[q] = s[q] + s[q]
        d[q] = d[q] + d[q]
    sxy_p, sxz_p, syz_p = s[7] + s[9], s[11] + s[13], s[15] + s[17]
    sxy, sxz, syz = s[7] - s[9], s[11] - s[13], s[15] - s[17]
    s0 = 12.0 * b[0] + (s[1] + s[3]) + (s[5] + sxy_p) + (sxz_p + syz_p)
    sxx, syy, szz = s[1] + sxy_p + sxz_p, s[3] + sxy_p + syz_p, s[5] + sxz_p + syz_p
    s1x = d[1] + (d[7] + d[9]) + (d[11] + d[13])
    s1y = d[3] + (d[7] - d[9]) + (d[15] + d[17])
    s1z = d[5] + (d[11] - d[13]) + (d[15] - d[17])
    tx = sxx * ux + sxy * uy + sxz * uz
    ty = sxy * ux + syy * uy + syz * uz
    tz = sxz * ux + syz * uy + szz * uz
    k = 1.6 / 36.0
    square = ux * ux + uy * uy + uz * uz
    level = k * (s0 * (1.0 + 1.5 * square) - 4.5 * (ux * tx + uy * ty + uz * tz))
    gx = (3.0 * k) * (s1x + 3.0 * tx - ux * s0)
    gy = (3.0 * k) * (s1y + 3.0 * ty - uy * s0)
    gz = (3.0 * k) * (s1z + 3.0 * tz - uz * s0)
    along = {
        1: gx,
        3: gy,
        5: gz,
        7: gx + gy,
        9: gx - gy,
        11: gx + gz,
        13: gx - gz,
        15: gy + gz,
        17: gy - gz,
    }
    result = [level - 0.6 * b[0]]
    for q in range(1, 19, 2):
        result.append((level + along[q]) - 0.6 * b[q])
        result.append((level - along[q]) - 0.6 * b[q + 1])
    return result


def forward_kernel(
    start_ref, fluid_ref, seed_ref,
    post_a, held, bits_ref,
    post_b, start, cells, solid, y_send, y_recv, c_send, c_recv,
    load_sem, send_sem, recv_sem,
):
    _, nx, ny, nz = start_ref.shape
    tiles = ny // T
    last = tiles - 1
    top = PAD + ny
    me = {"gx": lax.axis_index("gx"), "gy": lax.axis_index("gy")}
    count = {"gx": lax.axis_size("gx"), "gy": lax.axis_size("gy")}

    def device(dx, dy):
        to_x = lax.rem(me["gx"] + dx + count["gx"], count["gx"])
        to_y = lax.rem(me["gy"] + dy + count["gy"], count["gy"])
        return (to_x, to_y)

    around = [(i, j) for i in (-1, 0, 1) for j in (-1, 0, 1) if (i, j) != (0, 0)]
    barrier = pltpu.get_barrier_semaphore()

    fluid_load = pltpu.make_async_copy(fluid_ref, cells, load_sem.at[0])
    fluid_load.start()
    start_load = [
        pltpu.make_async_copy(start_ref.at[:, pl.ds(a, n)], start.at[:, pl.ds(a, n)], load_sem.at[1 + i])
        for i, (a, n) in enumerate(((0, 1), (nx - 1, 1), (1, nx - 2)))
    ]
    for load in start_load:
        load.start()
    seed_load = [
        pltpu.make_async_copy(
            seed_ref.at[q],
            held.at[SLOT[OPPOSITE[q]], pl.ds(1, nx), pl.ds(PAD, ny)],
            load_sem.at[4 + q],
        )
        for q in range(19)
    ]
    for load in seed_load:
        load.start()
    for i, j in around:
        pl.semaphore_signal(barrier, inc=1, device_id=device(i, j), device_id_type=pl.DeviceIdType.MESH)

    def copies(e, ref, is_cells):
        made = []
        for i, (plane, halo, first) in enumerate(((nx, 0, 1), (1, nx + 1, 6))):
            rows = pl.ds(PAD, ny)
            if is_cells:
                source, target = ref.at[plane, rows], ref.at[halo, rows]
            else:
                five = pl.ds(first, 5)
                source, target = ref.at[five, plane, rows], ref.at[five, halo, rows]
            made.append((source, target, device(1 - 2 * i, 0)))
        for i in range(2):
            made.append((y_send.at[e, i], y_recv.at[e, i], device(0, 1 - 2 * i)))
        for i, q in enumerate(CORNER):
            made.append((c_send.at[e, i], c_recv.at[e, i], device(VELOCITY[q][0], VELOCITY[q][1])))
        return [
            pltpu.make_async_remote_copy(
                src_ref=source, dst_ref=target, send_sem=send_sem.at[e, i], recv_sem=recv_sem.at[e, i],
                device_id=to, device_id_type=pl.DeviceIdType.MESH,
            )
            for i, (source, target, to) in enumerate(made)
        ]

    def pack(e, ref):
        def one(x, _):
            for k in range(5):
                y_send[e, 0, k, x] = ref[SLOT[UP[k]], x + 1, top - 1 : top, :]
                y_send[e, 1, k, x] = ref[SLOT[DOWN[k]], x + 1, PAD : PAD + 1, :]
            return 0

        lax.fori_loop(0, nx, one, 0)
        for i, q in enumerate(CORNER):
            plane = nx if VELOCITY[q][0] == 1 else 1
            row = top - 1 if VELOCITY[q][1] == 1 else PAD
            c_send[e, i] = ref[SLOT[q], plane, row : row + 1, :]

    def unpack(e, ref):
        def one(x, _):
            for k in range(5):
                ref[SLOT[UP[k]], x + 1, PAD - 1 : PAD, :] = y_recv[e, 0, k, x]
                ref[SLOT[DOWN[k]], x + 1, top : top + 1, :] = y_recv[e, 1, k, x]
            return 0

        lax.fori_loop(0, nx, one, 0)
        for i, q in enumerate(CORNER):
            plane = 0 if VELOCITY[q][0] == 1 else nx + 1
            row = PAD - 1 if VELOCITY[q][1] == 1 else top
            ref[SLOT[q], plane, row : row + 1, :] = c_recv[e, i]

    def sweep_rim(body):
        def face(i, _):
            for y in range(tiles):
                body(i * (nx - 1), y)
            return 0

        def edge(x, _):
            body(x, 0)
            body(x, last)
            return 0

        lax.fori_loop(0, 2, face, 0)
        lax.fori_loop(1, nx - 1, edge, 0)

    def sweep_interior(body):
        def line(x, _):
            for y in range(1, last):
                body(x, y)
            return 0

        lax.fori_loop(1, nx - 1, line, 0)

    def begin(made):
        for copy in made:
            copy.start()

    def finish(made):
        for copy in made:
            copy.wait()

    fluid_load.wait()

    def to_float(x, _):
        solid[x + 1, PAD:top, :] = cells[x].astype(jnp.float32)
        y_send[0, 0, 0, x] = solid[x + 1, top - 1 : top, :]
        y_send[0, 1, 0, x] = solid[x + 1, PAD : PAD + 1, :]
        for k in range(1, 5):
            y_send[0, 0, k, x] = jnp.zeros((1, nz), jnp.float32)
            y_send[0, 1, k, x] = jnp.zeros((1, nz), jnp.float32)
        return 0

    lax.fori_loop(0, nx, to_float, 0)
    for i, q in enumerate(CORNER):
        plane = nx if VELOCITY[q][0] == 1 else 1
        row = top - 1 if VELOCITY[q][1] == 1 else PAD
        c_send[0, i] = solid[plane, row : row + 1, :]
    pl.semaphore_wait(barrier, len(around))
    cell_copies = copies(0, solid, True)
    begin(cell_copies)

    def store(to, x, y, v, is_fluid):
        for q, value in enumerate(collide(v)):
            to[SLOT[q], x + 1, PAD + T * y : PAD + T * y + T, :] = jnp.where(
                is_fluid, value, v[OPPOSITE[q]]
            )

    def first(x, y):
        v = [start[q, x, T * y : T * y + T, :] for q in range(19)]
        store(post_a, x, y, v, solid[x + 1, PAD + T * y : PAD + T * y + T, :] > 0.5)

    for load in start_load:
        load.wait()
    sweep_rim(first)
    pack(1, post_a)
    first_copies = copies(1, post_a, False)
    begin(first_copies)
    sweep_interior(first)

    for load in seed_load:
        load.wait()
    pack(4, held)
    seed_copies = copies(4, held, False)
    begin(seed_copies)

    finish(cell_copies)

    def place_cells(x, _):
        solid[x + 1, PAD - 1 : PAD, :] = y_recv[0, 0, 0, x]
        solid[x + 1, top : top + 1, :] = y_recv[0, 1, 0, x]
        return 0

    lax.fori_loop(0, nx, place_cells, 0)
    for i, q in enumerate(CORNER):
        plane = 0 if VELOCITY[q][0] == 1 else nx + 1
        row = PAD - 1 if VELOCITY[q][1] == 1 else top
        solid[plane, row : row + 1, :] = c_recv[0, i]

    layer = lax.broadcasted_iota(jnp.int32, (T, nz), 1)
    inside = {1: (layer > 0).astype(jnp.float32), -1: (layer < nz - 1).astype(jnp.float32)}

    def mark(x, _):
        for y in range(tiles):
            flat, up, down = 1.0, 0.0, 0.0
            for q in range(1, 19):
                c = VELOCITY[q]
                row = PAD + T * y - c[1]
                tile = solid[x + 1 - c[0], row : row + T, :] * float(1 << q)
                if c[2] == 0:
                    flat = flat + tile
                elif c[2] == 1:
                    up = up + tile
                else:
                    down = down + tile
            total = flat + pltpu.roll(up, 1, 1) * inside[1] + pltpu.roll(down, nz - 1, 1) * inside[-1]
            here = solid[x + 1, PAD + T * y : PAD + T * y + T, :]
            bits_ref[x, T * y : T * y + T, :] = (total * here).astype(jnp.int32)
        return 0

    lax.fori_loop(0, nx, mark, 0)

    def middle(source, to):
        def body(x, y):
            bits = bits_ref[x, T * y : T * y + T, :]
            v = stream(source, bits, x, y)
            store(to, x, y, v, (bits & 1) != 0)

        return body

    sweep_interior(middle(post_a, post_b))
    finish(first_copies)
    unpack(1, post_a)
    sweep_rim(middle(post_a, post_b))
    pack(2, post_b)
    second_copies = copies(2, post_b, False)
    begin(second_copies)
    sweep_interior(middle(post_b, post_a))
    finish(second_copies)
    unpack(2, post_b)
    sweep_rim(middle(post_b, post_a))
    pack(3, post_a)
    third_copies = copies(3, post_a, False)
    begin(third_copies)
    finish(seed_copies)
    unpack(4, held)
    finish(third_copies)
    unpack(3, post_a)


def adjoint_kernel(post, held, bits_ref, state_ref, adjoint_ref):
    x = pl.program_id(0)
    tiles = bits_ref.shape[1] // T
    for y in range(tiles):
        rows = slice(T * y, T * y + T)
        bits = bits_ref[x, rows, :]
        v = stream(post, bits, x, y)
        for q in range(19):
            state_ref[q, 0, rows, :] = v[q]
        turned = stream(held, bits, x, y)
        b = [turned[OPPOSITE[q]] for q in range(19)]
        through = pull_back(v, b)
        is_fluid = (bits & 1) != 0
        for q in range(19):
            adjoint_ref[q, 0, rows, :] = jnp.where(is_fluid, through[q], turned[q])


def per_device(checkpoint, fluid, adjoint_in):
    n, nx, ny, nz = checkpoint.shape
    padded = (n, nx + 2, ny + 2 * PAD, nz)
    f32 = jnp.float32
    post, held, bits = pl.pallas_call(
        forward_kernel,
        out_shape=(
            pltpu.VMEM(padded, f32),
            pltpu.VMEM(padded, f32),
            pltpu.VMEM((nx, ny, nz), jnp.int32),
        ),
        in_specs=[pl.BlockSpec(memory_space=pl.ANY)] * 3,
        out_specs=[pl.BlockSpec(memory_space=pltpu.VMEM)] * 3,
        scratch_shapes=[
            pltpu.VMEM(padded, f32),
            pltpu.VMEM((n, nx, ny, nz), f32),
            pltpu.VMEM((nx, ny, nz), jnp.int32),
            pltpu.VMEM(padded[1:], f32),
            pltpu.VMEM((5, 2, 5, nx, 1, nz), f32),
            pltpu.VMEM((5, 2, 5, nx, 1, nz), f32),
            pltpu.VMEM((5, 4, 1, nz), f32),
            pltpu.VMEM((5, 4, 1, nz), f32),
            pltpu.SemaphoreType.DMA((23,)),
            pltpu.SemaphoreType.DMA((5, 8)),
            pltpu.SemaphoreType.DMA((5, 8)),
        ],
        compiler_params=pltpu.CompilerParams(
            collective_id=0, has_side_effects=True, vmem_limit_bytes=40 * MIB
        ),
        name="forward",
    )(checkpoint, fluid, adjoint_in)
    block = pl.BlockSpec((n, 1, ny, nz), lambda x: (0, x, 0, 0))
    return pl.pallas_call(
        adjoint_kernel,
        grid=(nx,),
        out_shape=(jax.ShapeDtypeStruct((n, nx, ny, nz), f32),) * 2,
        in_specs=[pl.BlockSpec(memory_space=pltpu.VMEM)] * 3,
        out_specs=(block, block),
        compiler_params=pltpu.CompilerParams(vmem_limit_bytes=12 * MIB),
        name="adjoint",
    )(post, held, bits)


def solution(mesh):
    return jax.shard_map(
        per_device,
        mesh=mesh,
        in_specs=(P(None, "gx", "gy", None), P("gx", "gy", None), P(None, "gx", "gy", None)),
        out_specs=(P(None, "gx", "gy", None), P(None, "gx", "gy", None)),
        check_vma=False,
    )
```

profile of v0, /device:TPU:0, one launch (start us, length us, event | category | flops | bytes accessed | tf_op | source)
XLA Modules:
  0.0 35.7 jit_solution(3863774703204565035)
XLA Ops:
  0.6 28.8 %forward.1 = (f32[19,10,80,128]{3,2,1,0:T(8,128)S(1)}, f32[19,10,80,128]{3,2,1,0:T(8,128)S(1)}, s32[8,64,128]{2,1,0:T(8,128)S(1)}) custom-call(f32[19,8,64,128]{3,2,1,0:T(8,128)} %start_ref.1, s32[8,64,128]{2,1,0:T(8,128)} %fluid_ref.1, f32[19,8,64,128]{3,2,1,0:T(8,128)} %seed_ref.1), custom_call_target="tpu_custom_call" | custom-call | tf_op jit(solution)/shard_map/forward/pallas_call | solution.py:391
  29.4 6.3 %adjoint.1 = (f32[19,8,64,128]{3,2,1,0:T(8,128)}, f32[19,8,64,128]{3,2,1,0:T(8,128)}) custom-call(f32[19,10,80,128]{3,2,1,0:T(8,128)S(1)} %get-tuple-element.5.post, f32[19,10,80,128]{3,2,1,0:T(8,128)S(1)} %get-tuple-element.6.held, s32[8,64,128]{2,1,0:T(8,128)S(1)} %get-tuple-element.7.bits_ref), custom_call_target="tpu_custom_call" | custom-call | tf_op jit(solution)/shard_map/adjoint/pallas_call | solution.py:419
where the time goes:
time: 35.9 us; the launch traced here: 35.7 us
  Pallas kernels  35.1 us (98%)
  between operations  0.64 us (2%)
    pallas_call x1, Pallas kernels, per_device(): pl.pallas_call(forward_kernel, out_shape=(pltpu.VMEM(padded, f32), pltpu....  28.8 us
    pallas_call x1, Pallas kernels, per_device(): pl.pallas_call(adjoint_kernel, grid=(nx,), out_shape=(jax.ShapeDtypeStruc...  6.27 us

commit v1 on v0

--- a/solution.py
+++ b/solution.py
@@ -141,8 +141,8 @@
 
 def forward_kernel(
     start_ref, fluid_ref, seed_ref,
-    post_a, held, bits_ref,
-    post_b, start, cells, solid, y_send, y_recv, c_send, c_recv,
+    state_ref, adjoint_ref,
+    post_a, held, bits_ref, post_b, start, cells, solid, y_send, y_recv, c_send, c_recv,
     load_sem, send_sem, recv_sem,
 ):
     _, nx, ny, nz = start_ref.shape
@@ -176,8 +176,6 @@
         )
         for q in range(19)
     ]
-    for load in seed_load:
-        load.start()
     for i, j in around:
         pl.semaphore_signal(barrier, inc=1, device_id=device(i, j), device_id_type=pl.DeviceIdType.MESH)
 
@@ -291,6 +289,8 @@
 
     for load in start_load:
         load.wait()
+    for load in seed_load:
+        load.start()
     sweep_rim(first)
     pack(1, post_a)
     first_copies = copies(1, post_a, False)
@@ -363,41 +363,52 @@
     begin(third_copies)
     finish(seed_copies)
     unpack(4, held)
+
+    def final(x, y):
+        rows = slice(T * y, T * y + T)
+        bits = bits_ref[x, rows, :]
+        v = stream(post_a, bits, x, y)
+        for q in range(19):
+            state_ref[q, x, rows, :] = v[q]
+        turned = stream(held, bits, x, y)
+        through = pull_back(v, [turned[OPPOSITE[q]] for q in range(19)])
+        is_fluid = (bits & 1) != 0
+        for q in range(19):
+            adjoint_ref[q, x, rows, :] = jnp.where(is_fluid, through[q], turned[q])
+
+    sweep_interior(final)
     finish(third_copies)
     unpack(3, post_a)
-
-
-def adjoint_kernel(post, held, bits_ref, state_ref, adjoint_ref):
-    x = pl.program_id(0)
-    tiles = bits_ref.shape[1] // T
-    for y in range(tiles):
-        rows = slice(T * y, T * y + T)
-        bits = bits_ref[x, rows, :]
-        v = stream(post, bits, x, y)
-        for q in range(19):
-            state_ref[q, 0, rows, :] = v[q]
-        turned = stream(held, bits, x, y)
-        b = [turned[OPPOSITE[q]] for q in range(19)]
-        through = pull_back(v, b)
-        is_fluid = (bits & 1) != 0
-        for q in range(19):
-            adjoint_ref[q, 0, rows, :] = jnp.where(is_fluid, through[q], turned[q])
+    sweep_rim(final)
+
+
+def write_kernel(state_in, adjoint_in, state_ref, adjoint_ref, sem):
+    made = []
+    for i, (source, target) in enumerate(((state_in, state_ref), (adjoint_in, adjoint_ref))):
+        for q in range(source.shape[0]):
+            made.append(pltpu.make_async_copy(source.at[q], target.at[q], sem.at[i, q]))
+    for copy in made:
+        copy.start()
+    for copy in made:
+        copy.wait()
 
 
 def per_device(checkpoint, fluid, adjoint_in):
     n, nx, ny, nz = checkpoint.shape
     padded = (n, nx + 2, ny + 2 * PAD, nz)
     f32 = jnp.float32
-    post, held, bits = pl.pallas_call(
+    state, adjoint = pl.pallas_call(
         forward_kernel,
         out_shape=(
+            pltpu.VMEM((n, nx, ny, nz), f32),
+            pltpu.VMEM((n, nx, ny, nz), f32),
+        ),
+        in_specs=[pl.BlockSpec(memory_space=pltpu.HBM)] * 3,
+        out_specs=[pl.BlockSpec(memory_space=pltpu.VMEM)] * 2,
+        scratch_shapes=[
             pltpu.VMEM(padded, f32),
             pltpu.VMEM(padded, f32),
             pltpu.VMEM((nx, ny, nz), jnp.int32),
-        ),
-        in_specs=[pl.BlockSpec(memory_space=pl.ANY)] * 3,
-        out_specs=[pl.BlockSpec(memory_space=pltpu.VMEM)] * 3,
-        scratch_shapes=[
             pltpu.VMEM(padded, f32),
             pltpu.VMEM((n, nx, ny, nz), f32),
             pltpu.VMEM((nx, ny, nz), jnp.int32),
@@ -411,20 +422,19 @@
             pltpu.SemaphoreType.DMA((5, 8)),
         ],
         compiler_params=pltpu.CompilerParams(
-            collective_id=0, has_side_effects=True, vmem_limit_bytes=40 * MIB
+            collective_id=0, has_side_effects=True, vmem_limit_bytes=44 * MIB
         ),
         name="forward",
     )(checkpoint, fluid, adjoint_in)
-    block = pl.BlockSpec((n, 1, ny, nz), lambda x: (0, x, 0, 0))
     return pl.pallas_call(
-        adjoint_kernel,
-        grid=(nx,),
+        write_kernel,
         out_shape=(jax.ShapeDtypeStruct((n, nx, ny, nz), f32),) * 2,
-        in_specs=[pl.BlockSpec(memory_space=pltpu.VMEM)] * 3,
-        out_specs=(block, block),
-        compiler_params=pltpu.CompilerParams(vmem_limit_bytes=12 * MIB),
-        name="adjoint",
-    )(post, held, bits)
+        in_specs=[pl.BlockSpec(memory_space=pltpu.VMEM)] * 2,
+        out_specs=[pl.BlockSpec(memory_space=pl.ANY)] * 2,
+        scratch_shapes=[pltpu.SemaphoreType.DMA((2, n))],
+        compiler_params=pltpu.CompilerParams(vmem_limit_bytes=4 * MIB),
+        name="write",
+    )(state, adjoint)
 
 
 def solution(mesh):

time: 35.9 us -> 36.3 us (1.011)
  local copies, waits for them, and re-layouts: 0 us -> 0.94 us
  Pallas kernels: 35.1 us -> 34.6 us
    unnamed x0 -> x2, local copies, waits for them, and re-layouts: none -> 0.94 us
    pallas_call x2, Pallas kernels: 35.1 us -> 34.6 us  [the longest x1 30.5 us: per_device(): pl.pallas_call(forward_kernel, out_shape=(pltpu.VMEM((n, nx, ny, nz), f32...]
where the time goes in v1:
time: 36.3 us; the launch traced here: 36.2 us
  Pallas kernels  34.6 us (95%)
  local copies, waits for them, and re-layouts  0.94 us (3%)
  between operations  0.65 us (2%)
    pallas_call x1, Pallas kernels, per_device(): pl.pallas_call(forward_kernel, out_shape=(pltpu.VMEM((n, nx, ny, nz), f32...  30.5 us
    pallas_call x1, Pallas kernels, per_device(): pl.pallas_call(write_kernel, out_shape=(jax.ShapeDtypeStruct((n, nx, ny,...  4.07 us
    unnamed x2, local copies, waits for them, and re-layouts  0.94 us

profile of v1, /device:TPU:0, one launch (start us, length us, event | category | flops | bytes accessed | tf_op | source)
XLA Modules:
  0.0 36.2 jit_solution(13296880030441722800)
XLA Ops:
  0.6 0.0 copy-start
  0.6 0.9 %copy-done = s32[8,64,128]{2,1,0:T(8,128)S(1)} copy-done((s32[8,64,128]{2,1,0:T(8,128)S(1)}, s32[8,64,128]{2,1,0:T(8,128)}, u32[]{:S(2)}) %copy-start) | copy-done | bytes 262168
  1.6 30.5 %forward.1 = (f32[19,8,64,128]{3,2,1,0:T(8,128)S(1)}, f32[19,8,64,128]{3,2,1,0:T(8,128)S(1)}) custom-call(f32[19,8,64,128]{3,2,1,0:T(8,128)} %start_ref.1, s32[8,64,128]{2,1,0:T(8,128)S(1)} %copy-done, f32[19,8,64,128]{3,2,1,0:T(8,128)} %seed_ref.1), custom_call_target="tpu_custom_call" | custom-call | tf_op jit(solution)/shard_map/forward/pallas_call | solution.py:400
  32.1 4.1 %write.1 = (f32[19,8,64,128]{3,2,1,0:T(8,128)}, f32[19,8,64,128]{3,2,1,0:T(8,128)}) custom-call(f32[19,8,64,128]{3,2,1,0:T(8,128)S(1)} %get-tuple-element.4.state_in, f32[19,8,64,128]{3,2,1,0:T(8,128)S(1)} %get-tuple-element.5.adjoint_in), custom_call_target="tpu_custom_call" | custom-call | tf_op jit(solution)/shard_map/write/pallas_call | solution.py:429
Async XLA Ops:
  0.6 1.0 %copy-start = (s32[8,64,128]{2,1,0:T(8,128)S(1)}, s32[8,64,128]{2,1,0:T(8,128)}, u32[]{:S(2)}) copy-start(s32[8,64,128]{2,1,0:T(8,128)} %fluid_ref.1) | copy-start | bytes 786436

commit v2 on v1

--- a/solution.py
+++ b/solution.py
@@ -143,7 +143,7 @@
     start_ref, fluid_ref, seed_ref,
     state_ref, adjoint_ref,
     post_a, held, bits_ref, post_b, start, cells, solid, y_send, y_recv, c_send, c_recv,
-    load_sem, send_sem, recv_sem,
+    load_sem, send_sem, recv_sem, seed_send, seed_recv,
 ):
     _, nx, ny, nz = start_ref.shape
     tiles = ny // T
@@ -159,6 +159,8 @@
 
     around = [(i, j) for i in (-1, 0, 1) for j in (-1, 0, 1) if (i, j) != (0, 0)]
     barrier = pltpu.get_barrier_semaphore()
+    for i, j in around:
+        pl.semaphore_signal(barrier, inc=1, device_id=device(i, j), device_id_type=pl.DeviceIdType.MESH)
 
     fluid_load = pltpu.make_async_copy(fluid_ref, cells, load_sem.at[0])
     fluid_load.start()
@@ -176,10 +178,25 @@
         )
         for q in range(19)
     ]
-    for i, j in around:
-        pl.semaphore_signal(barrier, inc=1, device_id=device(i, j), device_id_type=pl.DeviceIdType.MESH)
-
-    def copies(e, ref, is_cells):
+    pl.semaphore_wait(barrier, len(around))
+    seed_faces = []
+    for i, (plane, halo, first_slot) in enumerate(((nx - 1, 0, 1), (0, nx + 1, 6))):
+        for k in range(5):
+            slot = first_slot + k
+            seed_faces.append(
+                pltpu.make_async_remote_copy(
+                    src_ref=seed_ref.at[OPPOSITE[ORDER[slot]], plane],
+                    dst_ref=held.at[slot, halo, pl.ds(PAD, ny)],
+                    send_sem=seed_send.at[i, k],
+                    recv_sem=seed_recv.at[i, k],
+                    device_id=device(1 - 2 * i, 0),
+                    device_id_type=pl.DeviceIdType.MESH,
+                )
+            )
+    for copy in seed_faces:
+        copy.start()
+
+    def copies(e, ref, is_cells, first_of=0):
         made = []
         for i, (plane, halo, first) in enumerate(((nx, 0, 1), (1, nx + 1, 6))):
             rows = pl.ds(PAD, ny)
@@ -199,6 +216,7 @@
                 device_id=to, device_id_type=pl.DeviceIdType.MESH,
             )
             for i, (source, target, to) in enumerate(made)
+            if i >= first_of
         ]
 
     def pack(e, ref):
@@ -227,18 +245,20 @@
             row = PAD - 1 if VELOCITY[q][1] == 1 else top
             ref[SLOT[q], plane, row : row + 1, :] = c_recv[e, i]
 
-    def sweep_rim(body):
+    def sweep_faces(body):
         def face(i, _):
             for y in range(tiles):
                 body(i * (nx - 1), y)
             return 0
 
+        lax.fori_loop(0, 2, face, 0)
+
+    def sweep_edges(body):
         def edge(x, _):
             body(x, 0)
             body(x, last)
             return 0
 
-        lax.fori_loop(0, 2, face, 0)
         lax.fori_loop(1, nx - 1, edge, 0)
 
     def sweep_interior(body):
@@ -273,7 +293,6 @@
         plane = nx if VELOCITY[q][0] == 1 else 1
         row = top - 1 if VELOCITY[q][1] == 1 else PAD
         c_send[0, i] = solid[plane, row : row + 1, :]
-    pl.semaphore_wait(barrier, len(around))
     cell_copies = copies(0, solid, True)
     begin(cell_copies)
 
@@ -287,20 +306,23 @@
         v = [start[q, x, T * y : T * y + T, :] for q in range(19)]
         store(post_a, x, y, v, solid[x + 1, PAD + T * y : PAD + T * y + T, :] > 0.5)
 
-    for load in start_load:
+    for load in start_load[:2]:
         load.wait()
+    first_copies = copies(1, post_a, False)
+    sweep_faces(first)
+    begin(first_copies[:2])
+    start_load[2].wait()
     for load in seed_load:
         load.start()
-    sweep_rim(first)
+    sweep_edges(first)
     pack(1, post_a)
-    first_copies = copies(1, post_a, False)
-    begin(first_copies)
+    begin(first_copies[2:])
     sweep_interior(first)
 
     for load in seed_load:
         load.wait()
     pack(4, held)
-    seed_copies = copies(4, held, False)
+    seed_copies = copies(4, held, False, 2)
     begin(seed_copies)
 
     finish(cell_copies)
@@ -347,20 +369,22 @@
 
         return body
 
-    sweep_interior(middle(post_a, post_b))
-    finish(first_copies)
-    unpack(1, post_a)
-    sweep_rim(middle(post_a, post_b))
-    pack(2, post_b)
-    second_copies = copies(2, post_b, False)
-    begin(second_copies)
-    sweep_interior(middle(post_b, post_a))
-    finish(second_copies)
-    unpack(2, post_b)
-    sweep_rim(middle(post_b, post_a))
-    pack(3, post_a)
-    third_copies = copies(3, post_a, False)
-    begin(third_copies)
+    def step(e, made, source, to):
+        body = middle(source, to)
+        sweep_interior(body)
+        finish(made[2:])
+        unpack(e, source)
+        sweep_edges(body)
+        finish(made[:2])
+        sweep_faces(body)
+        later = copies(e + 1, to, False)
+        begin(later[:2])
+        pack(e + 1, to)
+        begin(later[2:])
+        return later
+
+    second_copies = step(1, first_copies, post_a, post_b)
+    third_copies = step(2, second_copies, post_b, post_a)
     finish(seed_copies)
     unpack(4, held)
 
@@ -377,9 +401,12 @@
             adjoint_ref[q, x, rows, :] = jnp.where(is_fluid, through[q], turned[q])
 
     sweep_interior(final)
-    finish(third_copies)
+    finish(third_copies[2:])
     unpack(3, post_a)
-    sweep_rim(final)
+    sweep_edges(final)
+    finish(third_copies[:2])
+    finish(seed_faces)
+    sweep_faces(final)
 
 
 def write_kernel(state_in, adjoint_in, state_ref, adjoint_ref, sem):
@@ -420,9 +447,11 @@
             pltpu.SemaphoreType.DMA((23,)),
             pltpu.SemaphoreType.DMA((5, 8)),
             pltpu.SemaphoreType.DMA((5, 8)),
+            pltpu.SemaphoreType.DMA((2, 5)),
+            pltpu.SemaphoreType.DMA((2, 5)),
         ],
         compiler_params=pltpu.CompilerParams(
-            collective_id=0, has_side_effects=True, vmem_limit_bytes=44 * MIB
+            collective_id=0, has_side_effects=True, vmem_limit_bytes=50 * MIB
         ),
         name="forward",
     )(checkpoint, fluid, adjoint_in)

time: 36.3 us -> 35.8 us (0.986)
  local copies, waits for them, and re-layouts: 0.94 us -> 0 us
  Pallas kernels: 34.6 us -> 35 us
    unnamed x2 -> x0, local copies, waits for them, and re-layouts: 0.94 us -> none
    pallas_call x1, Pallas kernels: 30.5 us -> 30.9 us  [per_device(): pl.pallas_call(forward_kernel, out_shape=(pltpu.VMEM((n, nx, ny, nz), f32...]
where the time goes in v2:
time: 35.8 us; the launch traced here: 35.6 us
  Pallas kernels  35 us (98%)
  between operations  0.64 us (2%)
    pallas_call x1, Pallas kernels, per_device(): pl.pallas_call(forward_kernel, out_shape=(pltpu.VMEM((n, nx, ny, nz), f32...  30.9 us
    pallas_call x1, Pallas kernels, per_device(): pl.pallas_call(write_kernel, out_shape=(jax.ShapeDtypeStruct((n, nx, ny,...  4.07 us

profile of v2, /device:TPU:0, one launch (start us, length us, event | category | flops | bytes accessed | tf_op | source)
XLA Modules:
  0.0 35.6 jit_solution(6968136920216113757)
XLA Ops:
  0.6 30.9 %forward.1 = (f32[19,8,64,128]{3,2,1,0:T(8,128)S(1)}, f32[19,8,64,128]{3,2,1,0:T(8,128)S(1)}) custom-call(f32[19,8,64,128]{3,2,1,0:T(8,128)} %start_ref.1, s32[8,64,128]{2,1,0:T(8,128)} %fluid_ref.1, f32[19,8,64,128]{3,2,1,0:T(8,128)} %seed_ref.1), custom_call_target="tpu_custom_call" | custom-call | tf_op jit(solution)/shard_map/forward/pallas_call | solution.py:427
  31.5 4.1 %write.1 = (f32[19,8,64,128]{3,2,1,0:T(8,128)}, f32[19,8,64,128]{3,2,1,0:T(8,128)}) custom-call(f32[19,8,64,128]{3,2,1,0:T(8,128)S(1)} %get-tuple-element.4.state_in, f32[19,8,64,128]{3,2,1,0:T(8,128)S(1)} %get-tuple-element.5.adjoint_in), custom_call_target="tpu_custom_call" | custom-call | tf_op jit(solution)/shard_map/write/pallas_call | solution.py:458

commit v3 on v2

--- a/solution.py
+++ b/solution.py
@@ -193,8 +193,6 @@
                     device_id_type=pl.DeviceIdType.MESH,
                 )
             )
-    for copy in seed_faces:
-        copy.start()
 
     def copies(e, ref, is_cells, first_of=0):
         made = []
@@ -324,6 +322,8 @@
     pack(4, held)
     seed_copies = copies(4, held, False, 2)
     begin(seed_copies)
+    for copy in seed_faces:
+        copy.start()
 
     finish(cell_copies)
 

time: 35.8 us -> 33.8 us (0.944)
  Pallas kernels: 35 us -> 33 us
    pallas_call x1, Pallas kernels: 30.9 us -> 29 us  [per_device(): pl.pallas_call(forward_kernel, out_shape=(pltpu.VMEM((n, nx, ny, nz), f32...]
where the time goes in v3:
time: 33.8 us; the launch traced here: 33.7 us
  Pallas kernels  33 us (98%)
  between operations  0.64 us (2%)
    pallas_call x1, Pallas kernels, per_device(): pl.pallas_call(forward_kernel, out_shape=(pltpu.VMEM((n, nx, ny, nz), f32...  29 us
    pallas_call x1, Pallas kernels, per_device(): pl.pallas_call(write_kernel, out_shape=(jax.ShapeDtypeStruct((n, nx, ny,...  4.07 us

profile of v3, /device:TPU:0, one launch (start us, length us, event | category | flops | bytes accessed | tf_op | source)
XLA Modules:
  0.0 33.7 jit_solution(12304948727227154671)
XLA Ops:
  0.6 29.0 %forward.1 = (f32[19,8,64,128]{3,2,1,0:T(8,128)S(1)}, f32[19,8,64,128]{3,2,1,0:T(8,128)S(1)}) custom-call(f32[19,8,64,128]{3,2,1,0:T(8,128)} %start_ref.1, s32[8,64,128]{2,1,0:T(8,128)} %fluid_ref.1, f32[19,8,64,128]{3,2,1,0:T(8,128)} %seed_ref.1), custom_call_target="tpu_custom_call" | custom-call | tf_op jit(solution)/shard_map/forward/pallas_call | solution.py:427
  29.6 4.1 %write.1 = (f32[19,8,64,128]{3,2,1,0:T(8,128)}, f32[19,8,64,128]{3,2,1,0:T(8,128)}) custom-call(f32[19,8,64,128]{3,2,1,0:T(8,128)S(1)} %get-tuple-element.4.state_in, f32[19,8,64,128]{3,2,1,0:T(8,128)S(1)} %get-tuple-element.5.adjoint_in), custom_call_target="tpu_custom_call" | custom-call | tf_op jit(solution)/shard_map/write/pallas_call | solution.py:458
